TPU v7x, 256 devices: a whole 4x4x8 slice. The times are simulated.
256 devices in a mesh: gx: 8 (over y, core), gy: 32 (over x, z).
Axes of the slice: x: 4, y: 4, z: 8, core: 2. Of those that a mesh axis runs over, the one named last changes fastest.
Arguments:
- mode_fields: float32 [64, 512, 1024], P(None, 'gy', 'gx'), may hold values from -8 to 8
- mean_field: float32 [512, 1024], P('gy', 'gx'), may hold values from 0.5 to 2
- coefficients: float32 [64, 131072], P(None, ('gx', 'gy')), may hold values from -40 to 40
Outputs:
- new_modes: float32 [64, 512, 1024], P(None, 'gy', 'gx')
- new_mean: float32 [512, 1024], P('gy', 'gx')
- new_coefficients: float32 [64, 131072], P(None, ('gx', 'gy'))
All inputs are finite; a program needn't handle non-finite values.
Results may differ from a plain program's by a relative error of at most 0.0003.
Values sent between devices are 32-bit elements; how exact they have to be, the bound alone decides.
A program may use at most 128 MiB of HBM per device.

v0:
```python
import jax
import jax.numpy as jnp
import numpy as np
from jax import lax
from jax.sharding import PartitionSpec as P

NS_ITERS = 6


TIME_STEP = 0.02
VISCOSITY = 0.25
PRECISE = lax.Precision.HIGHEST


def padded_2(array, sides, width):
    for axis, dim in sides:
        size, length = (lax.axis_size(axis), array.shape[dim])
        up = [(i, (i + 1) % size) for i in range(size)]
        down = [(j, i) for i, j in up]
        last = lax.slice_in_dim(array, length - width, length, axis=dim)
        first = lax.slice_in_dim(array, 0, width, axis=dim)
        before = lax.ppermute(last, axis, up)
        after = lax.ppermute(first, axis, down)
        array = jnp.concatenate([before, array, after], axis=dim)
    return array


def matmul(left, right):
    return jnp.dot(left, right, precision=PRECISE)


def pair_index(extent):
    flat_pairs = np.arange(extent * extent)
    leading = flat_pairs // extent
    trailing = flat_pairs % extent
    return (leading, trailing)


def pair_rows(values):
    extent = values.shape[0]
    return (values[:, None, :] * values[None, :, :]).reshape(extent * extent, values.shape[1])


def inverse_root(covariance):
    identity = jnp.eye(covariance.shape[0], dtype=jnp.float32)
    scaling = jnp.sqrt(jnp.sum(covariance * covariance) + 1e-06)
    current = covariance / scaling
    inverse = identity
    for iteration in range(NS_ITERS):
        middle = 0.5 * (3.0 * identity - matmul(inverse, current))
        current = matmul(current, middle)
        inverse = matmul(middle, inverse)
    return inverse / jnp.sqrt(scaling)


def per_device(mode_fields, mean_field, coefficients):
    extent = mode_fields.shape[0]
    devices = lax.axis_size("gx") * lax.axis_size("gy")
    local_cells = mode_fields.shape[1] * mode_fields.shape[2]
    cell_count = local_cells * devices
    samples = coefficients.shape[1] * devices
    leading, trailing = pair_index(extent)
    stacked = jnp.concatenate([mean_field[None], mode_fields], axis=0)
    padded = padded_2(stacked, (("gx", 2), ("gy", 1)), 1)
    middle = padded[:, 1:-1, 1:-1]
    western = padded[:, 1:-1, :-2]
    eastern = padded[:, 1:-1, 2:]
    southern = padded[:, :-2, 1:-1]
    northern = padded[:, 2:, 1:-1]
    upwinded = (2.0 * middle - western - southern).reshape(extent + 1, local_cells)
    smoothed = (western + eastern + southern + northern - 4.0 * middle).reshape(
        extent + 1, local_cells
    )
    mean_flat = mean_field.reshape(local_cells)
    mean_gradient = upwinded[0]
    mean_smooth = smoothed[0]
    gradient = upwinded[1:]
    flattened = mode_fields.reshape(extent, local_cells)
    linear = -mean_flat * gradient - flattened * mean_gradient + VISCOSITY * smoothed[1:]
    coupling_part = matmul(flattened, linear.T)
    products = (flattened[:, None, :] * gradient[None, :, :]).reshape(extent * extent, local_cells)
    triad_full = -matmul(products, flattened.T)
    totals = lax.psum(jnp.sum(coefficients, axis=1), ("gx", "gy"))
    sample_mean = totals / samples
    centered = coefficients - sample_mean[:, None]
    pairs = pair_rows(centered)
    triads, coupling, covariance, third_moment = lax.psum(
        (triad_full, coupling_part, matmul(centered, centered.T), matmul(pairs, centered.T)),
        ("gx", "gy"),
    )
    covariance = covariance / samples
    third_moment = third_moment / samples
    triads = triads / cell_count
    coupling = coupling / cell_count
    weights = pairs - covariance[leading, trailing][:, None]
    quadratic = lax.dot_general(triads, weights, (((0,), (0,)), ((), ())), precision=PRECISE)
    new_coefficients = centered + TIME_STEP * (matmul(coupling, centered) + quadratic)
    weighted = matmul(covariance.T, flattened)
    new_mean = mean_flat + TIME_STEP * (
        -mean_flat * mean_gradient + VISCOSITY * mean_smooth - jnp.sum(weighted * gradient, axis=0)
    )
    moment_term = matmul(third_moment.reshape(extent, extent * extent), products)
    forcing = matmul(covariance, linear) - moment_term
    half_power = inverse_root(covariance)
    weighting = matmul(half_power, half_power)
    projection = lax.psum(matmul(forcing, flattened.T), ("gx", "gy")) / cell_count
    residual = forcing - matmul(projection, flattened)
    stepped = flattened + TIME_STEP * matmul(weighting, residual)
    gram_matrix = lax.psum(matmul(stepped, stepped.T), ("gx", "gy")) / cell_count
    factor = jnp.linalg.cholesky(gram_matrix)
    new_modes = lax.linalg.triangular_solve(factor, stepped, left_side=True, lower=True)
    return (
        new_modes.reshape(mode_fields.shape),
        new_mean.reshape(mean_field.shape),
        new_coefficients,
    )


def solution(mesh):
    placed = (P(None, "gy", "gx"), P("gy", "gx"), P(None, ("gx", "gy")))
    return jax.shard_map(
        per_device,
        mesh=mesh,
        in_specs=placed,
        out_specs=(P(None, "gy", "gx"), P("gy", "gx"), P(None, ("gx", "gy"))),
        check_vma=False,
    )
```

profile of v0, /device:TPU:1, one launch (start us, length us, event | category | flops | bytes accessed | tf_op | source)
XLA Modules:
  0.0 718.7 jit_solution(3144528498174359174)
XLA Ops:
  7.2 1.4 fusion.14
  8.9 3.2 collective-permute-start.1
  12.5 1.0 reduce_sum.29
  13.5 81.1 %psum.49 = f32[64]{0:T(128)S(1)} all-reduce(f32[64]{0:T(128)S(1)} %reduce_sum.29), channel_id=1, replica_groups=mesh['gx'=8,'gy'=32] {'gx','gy'}, use_global_device_ids=true, to_apply=%region_1.0 | all-reduce | flops 64 | bytes 512 | tf_op jit(solution)/shard_map/psum | solution.py:83
  94.6 1.0 broadcast_subtract_fusion
  95.9 72.8 %psum.50 = f32[64,64]{1,0:T(8,128)S(1)} all-reduce(f32[64,64]{1,0:T(8,128)S(1)} %fusion.53), channel_id=1, replica_groups=mesh['gx'=8,'gy'=32] {'gx','gy'}, use_global_device_ids=true, to_apply=%region_2.0 | all-reduce | flops 4096 | bytes 32768 | tf_op jit(solution)/shard_map/psum | solution.py:87
  172.0 1.1 broadcast_multiply_fusion.1
  173.5 2.9 copy-done.2
  176.3 9.2 %fusion.63 = f32[4096,64]{0,1:T(8,128)} fusion(f32[4096,512]{1,0:T(8,128)S(1)} %bitcast.126, f32[64,512]{1,0:T(8,128)S(1)} %broadcast_subtract_fusion), kind=kOutput, calls=%fused_computation.121 | convolution fusion | flops 1610612736 | bytes 9568256 | tf_op jit(solution)/shard_map/dot_general | solution.py:29
  186.9 2.4 collective-permute-start.2
  189.7 3.1 collective-permute-start.3
  192.8 1.2 collective-permute-done.2
  194.4 0.9 fusion.17
  195.4 1.0 subtract_add_fusion
  196.5 11.6 %broadcast_multiply_fusion = f32[64,64,2048]{2,1,0:T(8,128)} fusion(f32[64,2048]{1,0:T(8,128)S(1)} %bitcast.132, f32[64,2048]{1,0:T(8,128)S(1)} %bitcast.131), kind=kLoop, calls=%fused_computation.1 | loop fusion | flops 8388608 | bytes 34603008 | tf_op jit(solution)/shard_map/mul | solution.py:81
  208.0 37.1 %convolution_negate_fusion = f32[4096,64]{0,1:T(8,128)} fusion(f32[4096,2048]{1,0:T(8,128)} %bitcast.117, f32[8,8,16,128]{3,2,1,0:T(8,128)S(1)} %bitcast.120), kind=kOutput, calls=%fused_computation.4 | convolution fusion | flops 6442713088 | bytes 35127296 | tf_op jit(solution)/shard_map/dot_general | solution.py:29
  245.3 26.7 %gather_fusion = f32[4096]{0:T(1024)S(1)} fusion(f32[64,64]{1,0:T(8,128)S(1)} %get-tuple-element.28, s32[4096]{0:T(1024)S(1)} %copy-done), kind=kCustom, calls=%fused_computation | custom fusion | bytes 65536 | tf_op jit(solution)/shard_map/gather | solution.py:95
  272.2 0.8 convolution_bitcast_fusion
  273.0 0.8 fusion.4
  274.5 1.1 fusion.22
  275.6 228.4 %all-reduce.4.cloned.1.call-done = (f32[4096,64]{0,1:T(8,128)}, f32[4096,64]{0,1:T(8,128)}) async-done(((f32[4096,64]{0,1:T(8,128)}, f32[4096,64]{0,1:T(8,128)}), (f32[4096,64]{0,1:T(8,128)}, f32[4096,64]{0,1:T(8,128)})) %all-reduce.4.cloned.1.call-update) | async-done | bytes 2097168 | tf_op jit(solution)/shard_map/psum | solution.py:87
  504.0 2.3 broadcast_multiply_fusion.2
  506.3 1.8 copy.55
  508.1 1.7 reshape.87
  509.8 24.4 %convolution_subtract_fusion = f32[64,2048]{1,0:T(8,128)S(1)} fusion(f32[64,2048]{1,0:T(8,128)S(1)} %fusion.22, f32[64,4096]{1,0:T(8,128)} %reshape.87, f32[4096,2048]{1,0:T(8,128)} %bitcast.118), kind=kOutput, calls=%fused_computation.7 | convolution fusion | flops 6442582016 | bytes 35651584 | tf_op jit(solution)/shard_map/dot_general | solution.py:29
  534.9 77.9 %psum.52 = f32[64,64]{0,1:T(8,128)S(1)} all-reduce(f32[64,64]{0,1:T(8,128)S(1)} %fusion.52), channel_id=1, replica_groups=mesh['gx'=8,'gy'=32] {'gx','gy'}, use_global_device_ids=true, to_apply=%region_5.0 | all-reduce | flops 4096 | bytes 32768 | tf_op jit(solution)/shard_map/psum | solution.py:106
  614.9 73.7 %all-reduce = (f32[64,64]{0,1:T(8,128)S(1)}, f32[64,64]{0,1:T(8,128)S(1)}) all-reduce(f32[64,64]{0,1:T(8,128)S(1)} %fusion.64, f32[64,64]{0,1:T(8,128)S(1)} %convolution_bitcast_fusion), channel_id=1, replica_groups=mesh['gx'=8,'gy'=32] {'gx','gy'}, use_global_device_ids=true, to_apply=%region_6.0 | all-reduce | flops 8192 | bytes 65536 | tf_op jit(solution)/shard_map/psum | solution.py:109
  688.7 5.8 cholesky.23
  695.9 4.9 custom-call.6
  701.4 1.1 copy.63
  702.5 7.9 %fusion = f32[64,512]{1,0:T(8,128)S(1)} fusion(f32[4096,512]{1,0:T(8,128)} %bitcast.127, f32[4096]{0:T(1024)S(1)} %gather_fusion, f32[4096,64]{0,1:T(8,128)S(1)} %copy-done.4), kind=kOutput, calls=%fused_computation.2 | convolution fusion | flops 1612972032 | bytes 9584640 | tf_op jit(solution)/shard_map/dot_general | solution.py:96
  710.5 1.0 fusion.6
  (60 shorter events, 11.7 us)
Async XLA Ops:
  7.2 496.8 %all-reduce.4.cloned.1.call-start = ((), (), s32[]{:S(2)}) async-start(), calls=%async_computation | async-start | bytes 4194304 | tf_op jit(solution)/shard_map/psum | solution.py:87
  8.9 177.1 %collective-permute-start.1 = (f32[65,16,1]{0,1,2:T(8,128)S(1)}, f32[65,16,1]{0,1,2:T(8,128)S(1)}, u32[]{:S(2)}, u32[]{:S(2)}) collective-permute-start(f32[65,16,1]{0,1,2:T(8,128)S(1)} %copy.51), channel_id=1, source_target_pairs={{32,0},{64,32},{96,64},{128,96},{160,128},{192,160},{224,192},{0,2... | collective-permute-start | bytes 12488 | tf_op jit(solution)/shard_map/ppermute | solution.py:23
  12.4 173.3 %collective-permute-start = (f32[65,16,1]{0,1,2:T(8,128)S(1)}, f32[65,16,1]{0,1,2:T(8,128)S(1)}, u32[]{:S(2)}, u32[]{:S(2)}) collective-permute-start(f32[65,16,1]{0,1,2:T(8,128)S(1)} %copy.49), channel_id=1, source_target_pairs={{0,32},{32,64},{64,96},{96,128},{128,160},{160,192},{192,224},{224... | collective-permute-start | bytes 12488 | tf_op jit(solution)/shard_map/ppermute | solution.py:22
  172.0 14.5 %copy-start.1 = (f32[64,16,128]{2,1,0:T(8,128)S(1)}, f32[64,16,128]{2,1,0:T(8,128)}, u32[]{:S(2)}) copy-start(f32[64,16,128]{2,1,0:T(8,128)} %param.7) | copy-start | bytes 1572868
  172.0 14.5 %copy-start.5 = (f32[16,128]{1,0:T(8,128)S(1)}, f32[16,128]{1,0:T(8,128)}, u32[]{:S(2)}) copy-start(f32[16,128]{1,0:T(8,128)} %param.8) | copy-start | bytes 24580
  173.1 3.2 copy-start.2
  186.9 7.0 collective-permute-start.2
  189.7 4.7 collective-permute-start.3
  208.0 37.3 %copy-start = (s32[4096]{0:T(1024)S(1)}, s32[4096]{0:T(1024)}, u32[]{:S(2)}) copy-start(s32[4096]{0:T(1024)} %constant.109) | copy-start | bytes 49156
  245.3 29.2 %copy-start.3 = (f32[64,16,128]{2,1,0:T(8,128)S(1)}, f32[64,16,128]{2,1,0:T(8,128)}, u32[]{:S(2)}) copy-start(f32[64,16,128]{2,1,0:T(8,128)} %get-tuple-element.22) | copy-start | bytes 1572868
  534.2 168.3 %copy-start.4 = (f32[4096,64]{0,1:T(8,128)S(1)}, f32[4096,64]{0,1:T(8,128)}, u32[]{:S(2)}) copy-start(f32[4096,64]{0,1:T(8,128)} %get-tuple-element.18) | copy-start | bytes 3145732
Sparse Core Ops, SparseCore 0:
  245.3 258.6 all-reduce.3
where the time goes:
time: 728 us; the launch traced here: 719 us
  blocking collectives  306 us (42%)
  waiting for transfers between devices  230 us (32%)
  matrix products  88.9 us (12%)
  local copies, waits for them, and re-layouts  35.8 us (5%)
  other arithmetic  34.5 us (5%)
  between operations  15.6 us (2%)
  starting transfers between devices  8.75 us (1%)
    psum x1, waiting for transfers between devices, per_device(): lax.psum((triad_full, coupling_part, matmul(centered, centered.T), matmul...  228 us
    psum x1, blocking collectives, per_device(): totals = lax.psum(jnp.sum(coefficients, axis=1), ('gx', 'gy'))  81.1 us
    dot_general x30, matrix products, matmul(): return jnp.dot(left, right, precision=PRECISE)  80.3 us
    psum x1, blocking collectives, per_device(): lax.psum(matmul(forcing, flattened.T), ('gx', 'gy')) / cell_count  77.9 us
    psum x1, blocking collectives, per_device(): lax.psum(matmul(stepped, stepped.T), ('gx', 'gy')) / cell_count  73.7 us
    psum x1, blocking collectives, per_device(): lax.psum((triad_full, coupling_part, matmul(centered, centered.T), matmul...  72.8 us
    gather x1, local copies, waits for them, and re-layouts, per_device(): weights = pairs - covariance[leading, trailing][:, None]  26.7 us
  transfers between devices with their start and end apart: 5, of which 2 were waited for; matrix products, arithmetic and copies ran while one was open for 7% of the time, Pallas kernels for 0%

commit v1 on v0

v1 whole, which is shorter than its diff:
```python
import functools

import jax
import jax.numpy as jnp
from jax import lax
from jax.experimental import pallas as pl
from jax.experimental.pallas import tpu as pltpu
from jax.sharding import PartitionSpec as P

NS_ITERS = 6
TIME_STEP = 0.02
VISCOSITY = 0.25
M = 64
F32 = jnp.float32
BF16 = jnp.bfloat16
HIGHEST = lax.Precision.HIGHEST
MESH = pl.DeviceIdType.MESH
SIZES = {"c": 2, "y": 4, "x": 4, "z": 8}

BASES = [sum(8 * (M - 8 * b) for b in range(block)) for block in range(9)]
PAIRS = BASES[8]
HALF = PAIRS // 2
GROUPS = ((0,), (1,), (2, 3), (4, 5, 6, 7))
SMALL = M // 2
ROWS = 1280


def coordinates():
    gx, gy = lax.axis_index("gx"), lax.axis_index("gy")
    return {"c": gx % 2, "y": gx // 2, "x": gy // 8, "z": gy % 8}


def group_size(axes):
    size = 1
    for axis in axes:
        size *= SIZES[axis]
    return size


def member_id(axes, member, place):
    place = dict(place)
    for axis in reversed(axes):
        place[axis] = member % SIZES[axis]
        member = member // SIZES[axis]
    return (place["y"] * 2 + place["c"], place["x"] * 8 + place["z"])


def own_member(axes, place):
    index = 0
    for axis in axes:
        index = index * SIZES[axis] + place[axis]
    return index


class AllReduce:
    def __init__(self, place, buffer, result, stages, refs):
        self.place, self.buffer, self.result = place, buffer, result
        self.last_up = len(stages)
        self.steps = []
        base, size = 0, buffer.shape[0]
        at = 0
        back = []
        for axes, scatter in stages:
            n = group_size(axes)
            piece = size // n if scatter else size
            self.steps.append(("up", axes, scatter, base, piece, refs[at : at + 3]))
            at += 3
            if scatter:
                back.append((axes, base, piece))
                base = base + own_member(axes, place) * piece
            size = piece
        for axes, start, piece in reversed(back):
            self.steps.append(("down", axes, False, start, piece, refs[at : at + 2]))
            at += 2
        self.started = 0
        self.finished = 0
        self.copies = []

    @staticmethod
    def scratch(rows, stages):
        shapes = []
        size = rows
        back = []
        for axes, scatter in stages:
            n = group_size(axes)
            size = size // n if scatter else size
            shapes += [pltpu.VMEM((n - 1, size, 128), F32)] + [pltpu.SemaphoreType.DMA((n - 1,))] * 2
            if scatter:
                back.append(axes)
        for axes in reversed(back):
            shapes += [pltpu.SemaphoreType.DMA((group_size(axes) - 1,))] * 2
        return shapes

    def start(self):
        kind, axes, scatter, base, piece, refs = self.steps[self.started]
        self.started += 1
        n, me = group_size(axes), own_member(axes, self.place)
        send, recv = refs[-2], refs[-1]
        self.copies = []
        for offset in range(1, n):
            member = (me + offset) % n
            if kind == "up":
                at = base + member * piece if scatter else base
                source = self.buffer.at[pl.ds(pl.multiple_of(at, 8), piece)]
                target = refs[0].at[offset - 1]
            else:
                source = self.result.at[pl.ds(pl.multiple_of(base + me * piece, 8), piece)]
                target = source
            copy = pltpu.make_async_remote_copy(
                src_ref=source,
                dst_ref=target,
                send_sem=send.at[offset - 1],
                recv_sem=recv.at[offset - 1],
                device_id=member_id(axes, member, self.place),
                device_id_type=MESH,
            )
            copy.start()
            self.copies.append(copy)

    def finish(self):
        kind, axes, scatter, base, piece, refs = self.steps[self.finished]
        self.finished += 1
        for copy in self.copies:
            copy.wait_recv()
        for copy in self.copies:
            copy.wait_send()
        if kind == "up":
            at = base + own_member(axes, self.place) * piece if scatter else base
            rows = pl.ds(pl.multiple_of(at, 8), piece)
            total = self.buffer[rows]
            for slot in range(group_size(axes) - 1):
                total = total + refs[0][slot]
            if self.finished == self.last_up:
                self.result[rows] = total
            else:
                self.buffer[rows] = total

    def advance(self):
        self.finish()
        if self.started < len(self.steps):
            self.start()

    def drain(self):
        while self.finished < len(self.steps):
            self.advance()


BIG = (("c", True), ("xy", True), ("z", False))
TINY = (("c", False), ("xy", False), ("z", False))
MID = (("c", True), ("xy", False), ("z", False))


def dot(left, right, precision=None):
    return jnp.dot(left, right, preferred_element_type=F32, precision=precision)


def dot_nt(left, right, precision=None):
    return lax.dot_general(
        left, right, (((1,), (1,)), ((), ())), preferred_element_type=F32, precision=precision
    )


def split(values):
    high = values.astype(BF16)
    return high, (values - high.astype(F32)).astype(BF16)


def stack4(values):
    high, low = split(values)
    return jnp.concatenate([high, high, low, low], axis=0)


def lanes_of(shape):
    return lax.broadcasted_iota(jnp.int32, shape, len(shape) - 1)


def high_low(doubled):
    high = doubled.astype(BF16).astype(F32)
    return jnp.where(lanes_of(doubled.shape) < M, high, doubled - high).astype(BF16)


def twice(values):
    return jnp.concatenate([values, values], axis=1)


def pair_rows(values, blocks):
    rows = []
    for block in blocks:
        others = values[8 * block :]
        for i in range(8 * block, 8 * block + 8):
            rows.append(values[i : i + 1] * others)
    return jnp.concatenate(rows, axis=0)


def add_pairs(total_ref, values, weights, first=False):
    for blocks in GROUPS:
        rows = slice(BASES[blocks[0]], BASES[blocks[-1] + 1])
        high, low = split(pair_rows(values, blocks))
        part = dot_nt(high, weights) + dot_nt(low, weights)
        if first:
            total_ref[rows] = part
        else:
            total_ref[rows] += part


def pack(total_ref, small, buffer_ref, scale):
    for at in range(0, HALF, 128):
        top = total_ref[at : at + 128]
        bottom = total_ref[HALF + at : HALF + at + 128]
        top = top + pltpu.roll(top, M, 1)
        bottom = bottom + pltpu.roll(bottom, M, 1)
        buffer_ref[at : at + 128] = jnp.where(lanes_of(top.shape) < M, top, bottom) * scale
    buffer_ref[HALF : HALF + SMALL] = (
        jnp.where(lanes_of((SMALL, 128)) < M, small[:SMALL], small[SMALL:]) * scale
    )
    buffer_ref[HALF + SMALL :] = jnp.zeros((ROWS - HALF - SMALL, 128), F32)


def unpack_rows(packed):
    turned = pltpu.roll(packed, M, 1)
    left = lanes_of(packed.shape) < M
    return jnp.where(left, packed, turned), jnp.where(left, turned, packed)


def unpack_small(packed):
    top, bottom = unpack_rows(packed)
    return jnp.concatenate([top, bottom], axis=0)


def expand(buffer_ref, pairs_ref, full_ref):
    for at in range(0, HALF, 128):
        top, bottom = unpack_rows(buffer_ref[at : at + 128])
        pairs_ref[at : at + 128] = top
        pairs_ref[HALF + at : HALF + at + 128] = bottom
    for i in range(M):
        block = i // 8
        count = M - 8 * block
        start = BASES[block] + (i - 8 * block) * count
        full_ref[i * M + 8 * block : (i + 1) * M] = pairs_ref[start : start + count]
        for below in range(block):
            stride = M - 8 * below
            start = BASES[below] + i - 8 * below
            full_ref[i * M + 8 * below : i * M + 8 * below + 8] = pairs_ref[
                pl.ds(start, 8, stride=stride), :
            ]


def contract(parts_ref, stacked, factors, total):
    for chunk in range(8):
        left = parts_ref[chunk * 512 : (chunk + 1) * 512]
        inner = dot(twice(left), stacked)
        for i in range(8):
            at = chunk * 8 + i
            total = total + inner[i * M : (i + 1) * M] * factors[at : at + 1]
    return total


def newton_schulz(covariance):
    row = lax.broadcasted_iota(jnp.int32, (M, M), 0)
    identity = jnp.where(row == lanes_of((M, M)), 1.0, 0.0).astype(F32)
    square = jnp.sum(jnp.sum(covariance * covariance, axis=1, keepdims=True), axis=0, keepdims=True)
    scaling = jnp.sqrt(square + 1e-06)
    current = covariance / scaling
    inverse = identity
    for iteration in range(NS_ITERS):
        middle = 0.5 * (3.0 * identity - dot(inverse, current, HIGHEST))
        current = dot(current, middle, HIGHEST)
        inverse = dot(middle, inverse, HIGHEST)
    half_power = inverse / jnp.sqrt(scaling)
    return dot(half_power, half_power, HIGHEST)


def inverse_factor(gram):
    row = lax.broadcasted_iota(jnp.int32, (M, 2 * M), 0)
    lane = lanes_of((M, 2 * M))
    table = jnp.where(lane < M, gram, jnp.where(lane - M == row, 1.0, 0.0))
    pivots = jnp.ones((M, 1), F32)
    column_row = lax.broadcasted_iota(jnp.int32, (M, 1), 0)
    for k in range(M):
        pivot_row = table[k : k + 1]
        pivot = pivot_row[:, k : k + 1]
        factor = jnp.where(column_row > k, table[:, k : k + 1] / pivot, 0.0)
        pivots = jnp.where(column_row == k, pivot, pivots)
        table = table - factor * pivot_row
    return table[:, M:] * lax.rsqrt(pivots)


def kernel(cells, samples, modes_ref, mean_ref, coef_ref, out_modes, out_mean, out_coef, *scratch):
    (field, grad, linear, force, centered, pair_sum, pairs, full_t, full_q,
     t_parts, q_parts, q_high, q_low, halo_send, halo_recv, halo_ssem, halo_rsem,
     mean_buf, t_buf, q_buf, gram_buf, t_all, q_all, gram_all) = scratch[:24]
    refs = scratch[24:]
    place = coordinates()
    gx, gy = lax.axis_index("gx"), lax.axis_index("gy")
    barrier = pltpu.get_barrier_semaphore()
    around = [((gx + 1) % 8, gy), ((gx + 7) % 8, gy), (gx, (gy + 1) % 32), (gx, (gy + 31) % 32)]
    count = 0
    for axes in ("c", "xy", "z"):
        n, me = group_size(axes), own_member(axes, place)
        for offset in range(1, n):
            pl.semaphore_signal(
                barrier, inc=1, device_id=member_id(axes, (me + offset) % n, place), device_id_type=MESH
            )
            count += 1
    for neighbour in around:
        pl.semaphore_signal(barrier, inc=1, device_id=neighbour, device_id_type=MESH)
        count += 1

    reducers = []
    at = 0
    for buffer, result, stages in (
        (mean_buf, mean_buf, TINY),
        (t_buf, t_all, BIG),
        (q_buf, q_all, BIG),
        (gram_buf, gram_all, MID),
    ):
        shapes = AllReduce.scratch(buffer.shape[0], stages)
        reducers.append(AllReduce(place, buffer, result, stages, refs[at : at + len(shapes)]))
        at += len(shapes)
    mean_sum, t_sum, q_sum, gram_sum = reducers

    eye = lax.broadcasted_iota(jnp.int32, (M, 128), 0) == lanes_of((M, 128))
    sums = jnp.sum(coef_ref[...], axis=1, keepdims=True)
    mean_buf[...] = jnp.broadcast_to(
        jnp.sum(jnp.where(eye, sums, 0.0), axis=0, keepdims=True), (8, 128)
    )

    rows = 72
    lane = lanes_of((rows, 128))
    first = jnp.zeros((rows, 128), F32)
    last = jnp.zeros((rows, 128), F32)
    for y in range(16):
        field[y, :M] = modes_ref[y]
        field[y, M:] = jnp.broadcast_to(mean_ref[y : y + 1], (8, 128))
        here = field[y]
        first = jnp.where(lane == y, pltpu.roll(here, y, 1) if y else here, first)
        last = jnp.where(lane == y, pltpu.roll(here, y + 1, 1), last)
        inner = 2.0 * here - jnp.where(lane == 0, 0.0, pltpu.roll(here, 1, 1))
        if y:
            inner = inner - field[y - 1]
        grad[y] = inner
    halo_send[0] = last
    halo_send[1] = first
    halo_send[2] = field[15]
    halo_send[3] = field[0]

    pl.semaphore_wait(barrier, count)
    mean_sum.start()
    halos = []
    for side in range(4):
        copy = pltpu.make_async_remote_copy(
            src_ref=halo_send.at[side],
            dst_ref=halo_recv.at[side],
            send_sem=halo_ssem.at[side],
            recv_sem=halo_rsem.at[side],
            device_id=around[side],
            device_id_type=MESH,
        )
        copy.start()
        halos.append(copy)

    def wide(ref, t):
        return jnp.concatenate([ref[2 * t, :M], ref[2 * t + 1, :M]], axis=1)

    def triad_step(t, carry):
        add_pairs(pair_sum, wide(field, t), jnp.concatenate(split(wide(grad, t)), axis=0))
        return carry

    pair_sum[...] = jnp.zeros(pair_sum.shape, F32)
    lax.fori_loop(0, 3, triad_step, 0)
    mean_sum.advance()
    lax.fori_loop(3, 8, triad_step, 0)

    for copy in halos:
        copy.wait_recv()
    for copy in halos:
        copy.wait_send()
    west, east, south, north = halo_recv[0], halo_recv[1], halo_recv[2], halo_recv[3]
    edge = jnp.concatenate([field[0, :M], first[:M]], axis=1)
    beyond = jnp.concatenate([south[:M], jnp.where(lane < 16, west, 0.0)[:M]], axis=1)
    add_pairs(pair_sum, edge, jnp.concatenate(split(-beyond), axis=0))
    coupling = jnp.zeros((M, 128), F32)
    for y in range(16):
        here = field[y]
        from_west = pltpu.roll(west, (128 - y) % 128, 1) if y else west
        from_east = pltpu.roll(east, 127 - y, 1)
        below = field[y - 1] if y else south
        above = field[y + 1] if y < 15 else north
        left = jnp.where(lane == 0, from_west, pltpu.roll(here, 1, 1))
        right = jnp.where(lane == 127, from_east, pltpu.roll(here, 127, 1))
        up = 2.0 * here - left - below
        lap = left + right + below + above - 4.0 * here
        grad[y] = up
        mean = mean_ref[y : y + 1]
        mean_up = up[M : M + 1]
        line = -mean * up[:M] - here[:M] * mean_up + VISCOSITY * lap[:M]
        linear[y] = line
        out_mean[y : y + 1] = mean + TIME_STEP * (-mean * mean_up + VISCOSITY * lap[M : M + 1])
        coupling = coupling + dot_nt(here[:M], jnp.concatenate([line, line], axis=0), HIGHEST)
    pack(pair_sum, -coupling, q_buf, -1.0 / cells)
    mean_sum.advance()
    q_sum.start()
    mean_sum.finish()

    sample_mean = jnp.sum(jnp.where(eye, mean_buf[0:1], 0.0), axis=1, keepdims=True) / samples
    centered[...] = coef_ref[...] - sample_mean
    for t in range(2):
        values = centered[:, 256 * t : 256 * t + 256]
        add_pairs(pair_sum, values, jnp.concatenate(split(values), axis=0), first=t == 0)
    values = centered[...]
    second = dot_nt(values, jnp.concatenate([values, values], axis=0), HIGHEST)
    pack(pair_sum, second, t_buf, 1.0 / samples)
    t_sum.start()
    q_sum.advance()
    t_sum.advance()
    q_sum.advance()
    t_sum.advance()
    q_sum.advance()
    t_sum.advance()
    q_sum.advance()
    t_sum.advance()
    q_sum.finish()
    t_sum.finish()

    covariance = unpack_small(t_all[HALF : HALF + SMALL])
    coupled = unpack_small(q_all[HALF : HALF + SMALL])
    expand(t_all, pairs, full_t)
    expand(q_all, pairs, full_q)
    constant = jnp.zeros((M, 128), F32)
    for j in range(M):
        at = slice(j * M, (j + 1) * M)
        t_parts[at] = high_low(full_t[at])
        q_values = full_q[at]
        high, low = split(q_values)
        q_high[at] = high
        q_low[at] = low
        q_parts[at] = high_low(q_values)
        constant = constant + q_values * covariance[j : j + 1]
    constant = jnp.sum(jnp.where(lanes_of((M, 128)) < M, constant, 0.0), axis=1, keepdims=True)
    covariance_parts = twice(high_low(covariance))

    def force_step(t, carry):
        modes = wide(field, t)
        slope = wide(grad, t)
        stacked = stack4(modes)
        line = wide(linear, t)
        moment = contract(t_parts, stacked, slope, jnp.zeros((M, 256), F32))
        forcing = dot(covariance_parts, stack4(line)) - moment
        force[2 * t] = forcing[:, :128]
        force[2 * t + 1] = forcing[:, 128:]
        mixed = dot(covariance_parts, stacked) * slope
        row = TIME_STEP * jnp.sum(mixed, axis=0, keepdims=True)
        out_mean[pl.ds(2 * t, 1)] += -row[:, :128]
        out_mean[pl.ds(2 * t + 1, 1)] += -row[:, 128:]
        return carry

    lax.fori_loop(0, 8, force_step, 0)

    def project_step(k, total):
        at = pl.ds(pl.multiple_of(k * M, M), M)
        left = twice(t_parts[at])
        right = jnp.concatenate([q_high[at], q_low[at]], axis=1)
        return total + dot_nt(left, jnp.concatenate([right, right], axis=0))

    projection = lax.fori_loop(0, M, project_step, jnp.zeros((M, 128), F32))
    half = jnp.where(lanes_of((M, 128)) < M, covariance, 0.0)
    projection = projection + dot_nt(half, jnp.concatenate([coupled, coupled], axis=0), HIGHEST)
    weighting = newton_schulz(covariance[:, :M])
    weighting_parts = twice(high_low(twice(weighting)))
    projection_parts = twice(high_low(projection))

    def step_step(t, total):
        modes = wide(field, t)
        residual = wide(force, t) - dot(projection_parts, stack4(modes))
        stepped = modes + TIME_STEP * dot(weighting_parts, stack4(residual))
        force[2 * t] = stepped[:, :128]
        force[2 * t + 1] = stepped[:, 128:]
        return total + dot_nt(stepped, jnp.concatenate([stepped, stepped], axis=0), HIGHEST)

    gram = lax.fori_loop(0, 8, step_step, jnp.zeros((M, 128), F32))
    gram_buf[...] = jnp.where(lanes_of((SMALL, 128)) < M, gram[:SMALL], gram[SMALL:]) * (1.0 / cells)
    gram_sum.start()

    coupled_parts = twice(high_low(coupled))

    for t in range(2):
        values = centered[:, 256 * t : 256 * t + 256]
        stacked = stack4(values)
        total = contract(q_parts, stacked, values, dot(coupled_parts, stacked)) - constant
        out_coef[:, 256 * t : 256 * t + 256] = values + TIME_STEP * total

    gram_sum.drain()
    inverse = inverse_factor(unpack_small(gram_all[...]))

    def final_step(y, carry):
        out_modes[y] = dot(inverse, force[y], HIGHEST)
        return carry

    lax.fori_loop(0, 16, final_step, 0)


def per_device(mode_fields, mean_field, coefficients):
    devices = lax.axis_size("gx") * lax.axis_size("gy")
    cells = mode_fields.shape[1] * mode_fields.shape[2] * devices
    samples = coefficients.shape[1] * devices
    scratch = [
        pltpu.VMEM((16, 72, 128), F32),
        pltpu.VMEM((16, 72, 128), F32),
        pltpu.VMEM((16, M, 128), F32),
        pltpu.VMEM((16, M, 128), F32),
        pltpu.VMEM((M, 512), F32),
        pltpu.VMEM((PAIRS, 128), F32),
        pltpu.VMEM((PAIRS, 128), F32),
        pltpu.VMEM((M * M, 128), F32),
        pltpu.VMEM((M * M, 128), F32),
        pltpu.VMEM((M * M, 128), BF16),
        pltpu.VMEM((M * M, 128), BF16),
        pltpu.VMEM((M * M, 128), BF16),
        pltpu.VMEM((M * M, 128), BF16),
        pltpu.VMEM((4, 72, 128), F32),
        pltpu.VMEM((4, 72, 128), F32),
        pltpu.SemaphoreType.DMA((4,)),
        pltpu.SemaphoreType.DMA((4,)),
        pltpu.VMEM((8, 128), F32),
        pltpu.VMEM((ROWS, 128), F32),
        pltpu.VMEM((ROWS, 128), F32),
        pltpu.VMEM((SMALL, 128), F32),
        pltpu.VMEM((ROWS, 128), F32),
        pltpu.VMEM((ROWS, 128), F32),
        pltpu.VMEM((SMALL, 128), F32),
    ]
    for rows, stages in ((8, TINY), (ROWS, BIG), (ROWS, BIG), (SMALL, MID)):
        scratch += AllReduce.scratch(rows, stages)
    whole = pl.BlockSpec(memory_space=pltpu.VMEM)
    fields, new_mean, new_coefficients = pl.pallas_call(
        functools.partial(kernel, cells, samples),
        out_shape=(
            jax.ShapeDtypeStruct((16, M, 128), F32),
            jax.ShapeDtypeStruct(mean_field.shape, F32),
            jax.ShapeDtypeStruct(coefficients.shape, F32),
        ),
        in_specs=[whole] * 3,
        out_specs=(whole,) * 3,
        scratch_shapes=scratch,
        compiler_params=pltpu.CompilerParams(
            collective_id=0, has_side_effects=True, vmem_limit_bytes=56 * 2**20
        ),
    )(jnp.transpose(mode_fields, (1, 0, 2)), mean_field, coefficients)
    return jnp.transpose(fields, (1, 0, 2)), new_mean, new_coefficients


def solution(mesh):
    placed = (P(None, "gy", "gx"), P("gy", "gx"), P(None, ("gx", "gy")))
    return jax.shard_map(
        per_device, mesh=mesh, in_specs=placed, out_specs=placed, check_vma=False
    )
```

time: 728 us -> 111 us (0.15); the launches traced: 719 us -> 111 us
  blocking collectives: 306 us -> 0 us
  waiting for transfers between devices: 230 us -> 0 us
  Pallas kernels: 0 us -> 105 us
  matrix products: 88.9 us -> 0 us
  other arithmetic: 34.5 us -> 0 us
  local copies, waits for them, and re-layouts: 35.8 us -> 5.45 us
  between operations: 15.6 us -> 0.66 us
  starting transfers between devices: 8.75 us -> 0 us
    psum x4 -> x0, blocking collectives: 306 us -> none  [the longest x1 81.1 us: per_device(): totals = lax.psum(jnp.sum(coefficients, axis=1), ('gx', 'gy'))]
    psum x1 -> x0, waiting for transfers between devices: 228 us -> none  [per_device(): lax.psum((triad_full, coupling_part, matmul(centered, centered.T), matmul...]
    pallas_call x0 -> x1, Pallas kernels: none -> 105 us  [per_device(): pl.pallas_call(functools.partial(kernel, cells, samples), out_shape=(jax....]
    dot_general x31 -> x0, matrix products: 88.3 us -> none  [the longest x30 80.3 us: matmul(): return jnp.dot(left, right, precision=PRECISE)]
    gather x1 -> x0, local copies, waits for them, and re-layouts: 26.7 us -> none  [per_device(): weights = pairs - covariance[leading, trailing][:, None]]
    mul x2 -> x0, other arithmetic: 12.7 us -> none  [the longest x1 11.6 us: per_device(): flattened[:, None, :] * gradient[None, :, :]]
    another operation x5 -> x0, other arithmetic: 12.1 us -> none  [the longest x3 6.52 us: per_device(): factor = jnp.linalg.cholesky(gram_matrix)]
    ppermute x4 -> x0, starting transfers between devices: 8.71 us -> none  [the longest x2 6.33 us: padded_2(): after = lax.ppermute(first, axis, down)]
  transfers between devices with their start and end apart: 5 -> 0, of which waited for: 2 -> 0; matrix products, arithmetic and copies ran while one was open for 7% -> 0% of each run, Pallas kernels for 0% -> 0%
where the time goes in v1:
time: 111 us
  Pallas kernels  105 us (95%)
  local copies, waits for them, and re-layouts  5.45 us (5%)
    pallas_call x1, Pallas kernels, per_device(): pl.pallas_call(functools.partial(kernel, cells, samples), out_shape=(jax....  105 us
    unnamed x8, local copies, waits for them, and re-layouts  5.45 us

profile of v1, /device:TPU:1, one launch (start us, length us, event | category | flops | bytes accessed | tf_op | source)
XLA Modules:
  0.0 111.3 jit_solution(10685590099988170867)
XLA Ops:
  0.6 2.0 %copy.9 = f32[64,16,128]{2,0,1:T(8,128)} copy(f32[64,16,128]{2,1,0:T(8,128)} %param.3) | data formatting | bytes 1048576 | tf_op args[0]
  2.6 105.2 %shard_map.58 = (f32[16,64,128]{2,1,0:T(8,128)}, f32[16,128]{1,0:T(8,128)}, f32[64,512]{1,0:T(8,128)}) custom-call(f32[16,64,128]{2,1,0:T(8,128)} %bitcast.4, f32[16,128]{1,0:T(8,128)} %mean_ref.1, f32[64,512]{1,0:T(8,128)} %coef_ref.1), custom_call_target="tpu_custom_call" | custom-call | tf_op jit(solution)/shard_map/pallas_call | solution.py:535
  107.8 0.0 copy-start.1
  107.8 0.0 copy-start
  107.8 2.2 %copy.7 = f32[64,16,128]{2,1,0:T(8,128)} copy(f32[64,16,128]{2,0,1:T(8,128)} %bitcast.5) | data formatting | bytes 1048576
  110.0 0.0 copy-done.1
  110.0 0.6 copy.12
  110.6 0.0 copy-done
  110.6 0.7 copy.13
Async XLA Ops:
  107.8 2.2 %copy-start.1 = (f32[16,128]{1,0:T(8,128)S(1)}, f32[16,128]{1,0:T(8,128)}, u32[]{:S(2)}) copy-start(f32[16,128]{1,0:T(8,128)} %get-tuple-element.16) | copy-start | bytes 24580
  107.8 2.8 %copy-start = (f32[64,512]{1,0:T(8,128)S(1)}, f32[64,512]{1,0:T(8,128)}, u32[]{:S(2)}) copy-start(f32[64,512]{1,0:T(8,128)} %get-tuple-element.17) | copy-start | bytes 393220

commit v2 on v1

--- a/solution.py
+++ b/solution.py
@@ -255,41 +255,51 @@
     return total
 
 
-def newton_schulz(covariance):
+def gram_of(parts, others):
+    full = dot_nt(parts, others)
+    half = full[:M] + full[M:]
+    return half + pltpu.roll(half, M, 1)
+
+
+def identity_matrix():
     row = lax.broadcasted_iota(jnp.int32, (M, M), 0)
-    identity = jnp.where(row == lanes_of((M, M)), 1.0, 0.0).astype(F32)
-    square = jnp.sum(jnp.sum(covariance * covariance, axis=1, keepdims=True), axis=0, keepdims=True)
-    scaling = jnp.sqrt(square + 1e-06)
-    current = covariance / scaling
-    inverse = identity
-    for iteration in range(NS_ITERS):
-        middle = 0.5 * (3.0 * identity - dot(inverse, current, HIGHEST))
-        current = dot(current, middle, HIGHEST)
-        inverse = dot(middle, inverse, HIGHEST)
-    half_power = inverse / jnp.sqrt(scaling)
-    return dot(half_power, half_power, HIGHEST)
+    return jnp.where(row == lanes_of((M, M)), 1.0, 0.0).astype(F32)
 
 
 def inverse_factor(gram):
     row = lax.broadcasted_iota(jnp.int32, (M, 2 * M), 0)
     lane = lanes_of((M, 2 * M))
     table = jnp.where(lane < M, gram, jnp.where(lane - M == row, 1.0, 0.0))
-    pivots = jnp.ones((M, 1), F32)
-    column_row = lax.broadcasted_iota(jnp.int32, (M, 1), 0)
-    for k in range(M):
-        pivot_row = table[k : k + 1]
-        pivot = pivot_row[:, k : k + 1]
-        factor = jnp.where(column_row > k, table[:, k : k + 1] / pivot, 0.0)
-        pivots = jnp.where(column_row == k, pivot, pivots)
-        table = table - factor * pivot_row
-    return table[:, M:] * lax.rsqrt(pivots)
+    done = []
+    for block in range(M // 8):
+        height = M - 8 * block
+        row = lax.broadcasted_iota(jnp.int32, (height, 2 * M), 0)
+        columns = [
+            jnp.broadcast_to(table[:, 8 * block + j : 8 * block + j + 1], (height, 2 * M))
+            for j in range(8)
+        ]
+        head, tail = table[:8], table[8:]
+        scales = jnp.zeros((8, 2 * M), F32)
+        for j in range(8):
+            pivot = columns[j][j : j + 1]
+            factor = jnp.where(row > j, columns[j] * (1.0 / pivot), 0.0)
+            scales = jnp.where(row[:8] == j, lax.rsqrt(pivot), scales)
+            pivot_row = head[j : j + 1]
+            for later in range(j + 1, 8):
+                columns[later] = columns[later] - factor * columns[later][j : j + 1]
+            head = head - factor[:8] * pivot_row
+            if height > 8:
+                tail = tail - factor[8:] * pivot_row
+        done.append(head * scales)
+        table = tail
+    return pltpu.roll(jnp.concatenate(done, axis=0), M, 1)
 
 
 def kernel(cells, samples, modes_ref, mean_ref, coef_ref, out_modes, out_mean, out_coef, *scratch):
-    (field, grad, linear, force, centered, pair_sum, pairs, full_t, full_q,
+    (field, grad, linear, field_hl, force_hl, step_hl, centered, pair_sum, pairs, full_t, full_q,
      t_parts, q_parts, q_high, q_low, halo_send, halo_recv, halo_ssem, halo_rsem,
-     mean_buf, t_buf, q_buf, gram_buf, t_all, q_all, gram_all) = scratch[:24]
-    refs = scratch[24:]
+     mean_buf, t_buf, q_buf, gram_buf, t_all, q_all, gram_all) = scratch[:26]
+    refs = scratch[26:]
     place = coordinates()
     gx, gy = lax.axis_index("gx"), lax.axis_index("gy")
     barrier = pltpu.get_barrier_semaphore()
@@ -330,7 +340,12 @@
     first = jnp.zeros((rows, 128), F32)
     last = jnp.zeros((rows, 128), F32)
     for y in range(16):
-        field[y, :M] = modes_ref[y]
+        modes = modes_ref[pl.ds(y, M, stride=16), :]
+        field[y, :M] = modes
+        high, low = split(modes)
+        side = slice(128 * (y % 2), 128 * (y % 2) + 128)
+        field_hl[y // 2, :M, side] = high
+        field_hl[y // 2, M:, side] = low
         field[y, M:] = jnp.broadcast_to(mean_ref[y : y + 1], (8, 128))
         here = field[y]
         first = jnp.where(lane == y, pltpu.roll(here, y, 1) if y else here, first)
@@ -343,6 +358,16 @@
     halo_send[1] = first
     halo_send[2] = field[15]
     halo_send[3] = field[0]
+
+    def wide(ref, t):
+        return jnp.concatenate([ref[2 * t, :M], ref[2 * t + 1, :M]], axis=1)
+
+    def triad_step(t, carry):
+        add_pairs(pair_sum, wide(field, t), jnp.concatenate(split(wide(grad, t)), axis=0))
+        return carry
+
+    pair_sum[...] = jnp.zeros(pair_sum.shape, F32)
+    lax.fori_loop(0, 3, triad_step, 0)
 
     pl.semaphore_wait(barrier, count)
     mean_sum.start()
@@ -358,23 +383,15 @@
         )
         copy.start()
         halos.append(copy)
-
-    def wide(ref, t):
-        return jnp.concatenate([ref[2 * t, :M], ref[2 * t + 1, :M]], axis=1)
-
-    def triad_step(t, carry):
-        add_pairs(pair_sum, wide(field, t), jnp.concatenate(split(wide(grad, t)), axis=0))
-        return carry
-
-    pair_sum[...] = jnp.zeros(pair_sum.shape, F32)
-    lax.fori_loop(0, 3, triad_step, 0)
+    lax.fori_loop(3, 4, triad_step, 0)
     mean_sum.advance()
-    lax.fori_loop(3, 8, triad_step, 0)
+    lax.fori_loop(4, 8, triad_step, 0)
 
     for copy in halos:
         copy.wait_recv()
     for copy in halos:
         copy.wait_send()
+    mean_sum.advance()
     west, east, south, north = halo_recv[0], halo_recv[1], halo_recv[2], halo_recv[3]
     edge = jnp.concatenate([field[0, :M], first[:M]], axis=1)
     beyond = jnp.concatenate([south[:M], jnp.where(lane < 16, west, 0.0)[:M]], axis=1)
@@ -396,19 +413,22 @@
         line = -mean * up[:M] - here[:M] * mean_up + VISCOSITY * lap[:M]
         linear[y] = line
         out_mean[y : y + 1] = mean + TIME_STEP * (-mean * mean_up + VISCOSITY * lap[M : M + 1])
-        coupling = coupling + dot_nt(here[:M], jnp.concatenate([line, line], axis=0), HIGHEST)
+    for t in range(8):
+        line_hl = jnp.concatenate(split(wide(linear, t)), axis=0)
+        coupling = coupling + gram_of(field_hl[t], line_hl)
     pack(pair_sum, -coupling, q_buf, -1.0 / cells)
-    mean_sum.advance()
     q_sum.start()
     mean_sum.finish()
 
     sample_mean = jnp.sum(jnp.where(eye, mean_buf[0:1], 0.0), axis=1, keepdims=True) / samples
     centered[...] = coef_ref[...] - sample_mean
+    q_sum.advance()
+    second = jnp.zeros((M, 128), F32)
     for t in range(2):
         values = centered[:, 256 * t : 256 * t + 256]
-        add_pairs(pair_sum, values, jnp.concatenate(split(values), axis=0), first=t == 0)
-    values = centered[...]
-    second = dot_nt(values, jnp.concatenate([values, values], axis=0), HIGHEST)
+        values_hl = jnp.concatenate(split(values), axis=0)
+        add_pairs(pair_sum, values, values_hl, first=t == 0)
+        second = second + gram_of(values_hl, values_hl)
     pack(pair_sum, second, t_buf, 1.0 / samples)
     t_sum.start()
     q_sum.advance()
@@ -417,86 +437,108 @@
     t_sum.advance()
     q_sum.advance()
     t_sum.advance()
-    q_sum.advance()
-    t_sum.advance()
     q_sum.finish()
-    t_sum.finish()
-
-    covariance = unpack_small(t_all[HALF : HALF + SMALL])
-    coupled = unpack_small(q_all[HALF : HALF + SMALL])
-    expand(t_all, pairs, full_t)
     expand(q_all, pairs, full_q)
-    constant = jnp.zeros((M, 128), F32)
     for j in range(M):
         at = slice(j * M, (j + 1) * M)
-        t_parts[at] = high_low(full_t[at])
         q_values = full_q[at]
         high, low = split(q_values)
         q_high[at] = high
         q_low[at] = low
         q_parts[at] = high_low(q_values)
-        constant = constant + q_values * covariance[j : j + 1]
-    constant = jnp.sum(jnp.where(lanes_of((M, 128)) < M, constant, 0.0), axis=1, keepdims=True)
+    coupled = unpack_small(q_all[HALF : HALF + SMALL])
+    t_sum.drain()
+
+    covariance = unpack_small(t_all[HALF : HALF + SMALL])
+    expand(t_all, pairs, full_t)
+    for j in range(M):
+        at = slice(j * M, (j + 1) * M)
+        t_parts[at] = high_low(full_t[at])
     covariance_parts = twice(high_low(covariance))
 
+    square = jnp.where(lanes_of((M, 128)) < M, covariance * covariance, 0.0)
+    square = jnp.sum(jnp.sum(square, axis=1, keepdims=True), axis=0, keepdims=True)
+    scaling = jnp.sqrt(square + 1e-06)
+    identity = identity_matrix()
+
     def force_step(t, carry):
-        modes = wide(field, t)
+        projection, current, inverse = carry
+        high, low = field_hl[t, :M], field_hl[t, M:]
+        stacked = jnp.concatenate([high, high, low, low], axis=0)
         slope = wide(grad, t)
-        stacked = stack4(modes)
-        line = wide(linear, t)
         moment = contract(t_parts, stacked, slope, jnp.zeros((M, 256), F32))
-        forcing = dot(covariance_parts, stack4(line)) - moment
-        force[2 * t] = forcing[:, :128]
-        force[2 * t + 1] = forcing[:, 128:]
+        forcing = dot(covariance_parts, stack4(wide(linear, t))) - moment
+        high, low = split(forcing)
+        force_hl[t, :M] = high
+        force_hl[t, M:] = low
         mixed = dot(covariance_parts, stacked) * slope
         row = TIME_STEP * jnp.sum(mixed, axis=0, keepdims=True)
         out_mean[pl.ds(2 * t, 1)] += -row[:, :128]
         out_mean[pl.ds(2 * t + 1, 1)] += -row[:, 128:]
-        return carry
-
-    lax.fori_loop(0, 8, force_step, 0)
-
-    def project_step(k, total):
-        at = pl.ds(pl.multiple_of(k * M, M), M)
-        left = twice(t_parts[at])
-        right = jnp.concatenate([q_high[at], q_low[at]], axis=1)
-        return total + dot_nt(left, jnp.concatenate([right, right], axis=0))
-
-    projection = lax.fori_loop(0, M, project_step, jnp.zeros((M, 128), F32))
-    half = jnp.where(lanes_of((M, 128)) < M, covariance, 0.0)
-    projection = projection + dot_nt(half, jnp.concatenate([coupled, coupled], axis=0), HIGHEST)
-    weighting = newton_schulz(covariance[:, :M])
-    weighting_parts = twice(high_low(twice(weighting)))
-    projection_parts = twice(high_low(projection))
-
-    def step_step(t, total):
-        modes = wide(field, t)
-        residual = wide(force, t) - dot(projection_parts, stack4(modes))
-        stepped = modes + TIME_STEP * dot(weighting_parts, stack4(residual))
-        force[2 * t] = stepped[:, :128]
-        force[2 * t + 1] = stepped[:, 128:]
-        return total + dot_nt(stepped, jnp.concatenate([stepped, stepped], axis=0), HIGHEST)
-
-    gram = lax.fori_loop(0, 8, step_step, jnp.zeros((M, 128), F32))
+
+        lefts, rights = [], []
+        for k in range(8):
+            at = pl.ds(pl.multiple_of((8 * t + k) * M, M), M)
+            lefts += [t_parts[at]] * 2
+            rights += [q_high[at], q_low[at]]
+        projection = projection + dot_nt(
+            jnp.concatenate(lefts, axis=1), jnp.concatenate(rights, axis=1)
+        )
+
+        middle = 0.5 * (3.0 * identity - dot(inverse, current, HIGHEST))
+        live = t < NS_ITERS
+        next_current = jnp.where(live, dot(current, middle, HIGHEST), current)
+        next_inverse = jnp.where(live, dot(middle, inverse, HIGHEST), inverse)
+        return projection, next_current, next_inverse
+
+    start = covariance[:, :M] / scaling
+    projection, current, inverse = lax.fori_loop(
+        0, 8, force_step, (jnp.zeros((M, M), F32), start, identity)
+    )
+    projection = projection + dot_nt(covariance[:, :M], coupled[:, :M], HIGHEST)
+    half_power = inverse / jnp.sqrt(scaling)
+    weighting = dot(half_power, half_power, HIGHEST)
+    mixed = dot(weighting, projection, HIGHEST)
+    step_parts = jnp.concatenate(
+        [twice(high_low(twice(weighting))), twice(high_low(twice(-mixed)))], axis=1
+    )
+    gram = jnp.zeros((M, 128), F32)
+    for t in range(8):
+        high, low = force_hl[t, :M], force_hl[t, M:]
+        mode_high, mode_low = field_hl[t, :M], field_hl[t, M:]
+        stacked = jnp.concatenate(
+            [high, high, low, low, mode_high, mode_high, mode_low, mode_low], axis=0
+        )
+        stepped = wide(field, t) + TIME_STEP * dot(step_parts, stacked)
+        high, low = split(stepped)
+        step_hl[t, :M] = high
+        step_hl[t, M:] = low
+        both = jnp.concatenate([high, low], axis=0)
+        gram = gram + gram_of(both, both)
     gram_buf[...] = jnp.where(lanes_of((SMALL, 128)) < M, gram[:SMALL], gram[SMALL:]) * (1.0 / cells)
     gram_sum.start()
 
+    constant = jnp.zeros((M, 128), F32)
+    for j in range(M):
+        constant = constant + full_q[j * M : (j + 1) * M] * covariance[j : j + 1]
+    constant = jnp.sum(jnp.where(lanes_of((M, 128)) < M, constant, 0.0), axis=1, keepdims=True)
     coupled_parts = twice(high_low(coupled))
-
     for t in range(2):
+        if t:
+            gram_sum.advance()
         values = centered[:, 256 * t : 256 * t + 256]
         stacked = stack4(values)
         total = contract(q_parts, stacked, values, dot(coupled_parts, stacked)) - constant
         out_coef[:, 256 * t : 256 * t + 256] = values + TIME_STEP * total
 
     gram_sum.drain()
-    inverse = inverse_factor(unpack_small(gram_all[...]))
-
-    def final_step(y, carry):
-        out_modes[y] = dot(inverse, force[y], HIGHEST)
-        return carry
-
-    lax.fori_loop(0, 16, final_step, 0)
+    factor = inverse_factor(unpack_small(gram_all[...]))
+    factor_parts = twice(high_low(jnp.where(lanes_of((M, 128)) < M, factor, pltpu.roll(factor, M, 1))))
+    for t in range(8):
+        high, low = step_hl[t, :M], step_hl[t, M:]
+        result = dot(factor_parts, jnp.concatenate([high, high, low, low], axis=0))
+        out_modes[pl.ds(2 * t, M, stride=16), :] = result[:, :128]
+        out_modes[pl.ds(2 * t + 1, M, stride=16), :] = result[:, 128:]
 
 
 def per_device(mode_fields, mean_field, coefficients):
@@ -507,7 +549,9 @@
         pltpu.VMEM((16, 72, 128), F32),
         pltpu.VMEM((16, 72, 128), F32),
         pltpu.VMEM((16, M, 128), F32),
-        pltpu.VMEM((16, M, 128), F32),
+        pltpu.VMEM((8, 128, 256), BF16),
+        pltpu.VMEM((8, 128, 256), BF16),
+        pltpu.VMEM((8, 128, 256), BF16),
         pltpu.VMEM((M, 512), F32),
         pltpu.VMEM((PAIRS, 128), F32),
         pltpu.VMEM((PAIRS, 128), F32),
@@ -529,13 +573,13 @@
         pltpu.VMEM((ROWS, 128), F32),
         pltpu.VMEM((SMALL, 128), F32),
     ]
-    for rows, stages in ((8, TINY), (ROWS, BIG), (ROWS, BIG), (SMALL, MID)):
-        scratch += AllReduce.scratch(rows, stages)
+    for size, stages in ((8, TINY), (ROWS, BIG), (ROWS, BIG), (SMALL, MID)):
+        scratch += AllReduce.scratch(size, stages)
     whole = pl.BlockSpec(memory_space=pltpu.VMEM)
     fields, new_mean, new_coefficients = pl.pallas_call(
         functools.partial(kernel, cells, samples),
         out_shape=(
-            jax.ShapeDtypeStruct((16, M, 128), F32),
+            jax.ShapeDtypeStruct((16 * M, 128), F32),
             jax.ShapeDtypeStruct(mean_field.shape, F32),
             jax.ShapeDtypeStruct(coefficients.shape, F32),
         ),
@@ -545,8 +589,8 @@
         compiler_params=pltpu.CompilerParams(
             collective_id=0, has_side_effects=True, vmem_limit_bytes=56 * 2**20
         ),
-    )(jnp.transpose(mode_fields, (1, 0, 2)), mean_field, coefficients)
-    return jnp.transpose(fields, (1, 0, 2)), new_mean, new_coefficients
+    )(mode_fields.reshape(16 * M, 128), mean_field, coefficients)
+    return fields.reshape(mode_fields.shape), new_mean, new_coefficients
 
 
 def solution(mesh):

time: 111 us -> 81.9 us (0.74)
  Pallas kernels: 105 us -> 77.9 us
  local copies, waits for them, and re-layouts: 5.45 us -> 3.17 us
    pallas_call x1, Pallas kernels: 105 us -> 77.9 us  [per_device(): pl.pallas_call(functools.partial(kernel, cells, samples), out_shape=(jax....]
    unnamed x8 -> x7, local copies, waits for them, and re-layouts: 5.45 us -> 3.17 us
where the time goes in v2:
time: 81.9 us; the launch traced here: 81.8 us
  Pallas kernels  77.9 us (95%)
  local copies, waits for them, and re-layouts  3.17 us (4%)
    pallas_call x1, Pallas kernels, per_device(): pl.pallas_call(functools.partial(kernel, cells, samples), out_shape=(jax....  77.9 us
    unnamed x7, local copies, waits for them, and re-layouts  3.17 us

profile of v2, /device:TPU:1, one launch (start us, length us, event | category | flops | bytes accessed | tf_op | source)
XLA Modules:
  0.0 81.8 jit_solution(7557892993334620681)
XLA Ops:
  0.6 77.9 %shard_map.58 = (f32[1024,128]{1,0:T(8,128)}, f32[16,128]{1,0:T(8,128)}, f32[64,512]{1,0:T(8,128)}) custom-call(f32[1024,128]{1,0:T(8,128)} %bitcast.2, f32[16,128]{1,0:T(8,128)} %mean_ref.1, f32[64,512]{1,0:T(8,128)} %coef_ref.1), custom_call_target="tpu_custom_call" | custom-call | tf_op jit(solution)/shard_map/pallas_call | solution.py:579
  78.6 0.0 copy-start.1
  78.6 0.0 copy-start
  78.6 1.9 %copy.9 = f32[64,16,128]{2,1,0:T(8,128)} copy(f32[64,16,128]{2,1,0:T(8,128)} %bitcast.3) | data formatting | bytes 1048576
  80.5 0.0 copy-done.1
  80.5 0.6 copy.10
  81.1 0.0 copy-done
  81.1 0.7 copy.11
Async XLA Ops:
  78.6 1.9 %copy-start.1 = (f32[16,128]{1,0:T(8,128)S(1)}, f32[16,128]{1,0:T(8,128)}, u32[]{:S(2)}) copy-start(f32[16,128]{1,0:T(8,128)} %get-tuple-element.13) | copy-start | bytes 24580
  78.6 2.5 %copy-start = (f32[64,512]{1,0:T(8,128)S(1)}, f32[64,512]{1,0:T(8,128)}, u32[]{:S(2)}) copy-start(f32[64,512]{1,0:T(8,128)} %get-tuple-element.14) | copy-start | bytes 393220
